TPU v7x, 256 devices: a whole 4x4x8 slice. The times are simulated.
256 devices in a mesh: dp: 16 (over x_hi, y, core), tensor: 16 (over z, x_lo).
Axes of the slice: x: 4 (x_hi: 2, x_lo: 2; x = x_hi * 2 + x_lo), y: 4, z: 8, core: 2. Of those that a mesh axis runs over, the one named last changes fastest.
Arguments:
- activations: bfloat16 [2048, 4096], P(('dp', 'tensor')), may hold values from -24 to 24
- gate_pre: bfloat16 [2048, 14336], P('dp', 'tensor'), may hold values from -6 to 6
- up_pre: bfloat16 [2048, 14336], P('dp', 'tensor'), may hold values from -6 to 6
- hidden_grad: bfloat16 [2048, 14336], P('dp', 'tensor'), may hold values from -6 to 6
- gate_weight: bfloat16 [4096, 14336], P('dp', 'tensor'), may hold values from -0.09375 to 0.09375
- up_weight: bfloat16 [4096, 14336], P('dp', 'tensor'), may hold values from -0.09375 to 0.09375
Outputs:
- input_grad: bfloat16 [2048, 4096], P(('dp', 'tensor'))
- gate_weight_grad: bfloat16 [4096, 14336], P('dp', 'tensor')
- up_weight_grad: bfloat16 [4096, 14336], P('dp', 'tensor')
All inputs are finite; a program needn't handle non-finite values.
Results may differ from a plain program's by a relative error of at most 0.024.
Values may be sent and summed in bfloat16 or wider, within the bound.
A program may use at most 128 MiB of HBM per device.

v0:
```python
import jax
import jax.numpy as jnp
from jax import lax
from jax.sharding import PartitionSpec as P


def body(activations, gate_pre, up_pre, hidden_grad, gate_weight, up_weight):
    gate_value = gate_pre.astype(jnp.float32)
    up_value = up_pre.astype(jnp.float32)
    upstream = hidden_grad.astype(jnp.float32)
    gate_sigmoid = jax.nn.sigmoid(gate_value)
    grad_up = (upstream * gate_value * gate_sigmoid).astype(jnp.bfloat16)
    grad_gate = (
        upstream * up_value * gate_sigmoid * (1.0 + gate_value * (1.0 - gate_sigmoid))
    ).astype(jnp.bfloat16)
    both_grads = jnp.concatenate((grad_gate, grad_up), axis=1)
    both_weights = jnp.concatenate((gate_weight, up_weight), axis=1)
    features = lax.all_gather(activations, "tensor", axis=0, tiled=True)
    terms = lax.dot_general(
        both_grads,
        lax.all_gather(both_weights, "dp", axis=0, tiled=True),
        (((1,), (1,)), ((), ())),
        preferred_element_type=jnp.float32,
    )
    input_grad = lax.psum_scatter(
        terms.astype(jnp.bfloat16), "tensor", scatter_dimension=0, tiled=True
    )
    group_tokens = features.shape[0]
    grad_scale = float(group_tokens * lax.axis_size("dp")) ** (-0.5)
    width = gate_weight.shape[1]
    summed = lax.psum_scatter(
        (
            lax.dot_general(
                features, both_grads, (((0,), (0,)), ((), ())), preferred_element_type=jnp.float32
            )
            * grad_scale
        ).astype(jnp.bfloat16),
        "dp",
        scatter_dimension=0,
        tiled=True,
    )
    return (input_grad, summed[:, :width], summed[:, width:])


def solution(mesh):
    in_specs = (
        P(("dp", "tensor"), None),
        P("dp", "tensor"),
        P("dp", "tensor"),
        P("dp", "tensor"),
        P("dp", "tensor"),
        P("dp", "tensor"),
    )
    out_specs = (P(("dp", "tensor"), None), P("dp", "tensor"), P("dp", "tensor"))
    return jax.shard_map(body, mesh=mesh, in_specs=in_specs, out_specs=out_specs, check_vma=False)
```

profile of v0, /device:TPU:8, one launch (start us, length us, event | category | flops | bytes accessed | tf_op | source)
XLA Modules:
  0.0 411.3 jit_solution(1565563252406689038)
XLA Ops:
  7.2 0.0 all-gather.5.cloned.1.call-start
  7.2 0.7 all-gather.5.cloned.1.call-update
  7.9 0.0 all-gather.3.cloned.1.call-start
  7.9 2.1 pad_maximum_fusion
  10.1 0.0 all-gather.3.cloned.1.call-update
  10.1 0.0 reduce-scatter.5.cloned.1.call-start
  10.2 1.4 fusion.3
  11.6 69.8 %all-gather.5.cloned.1.call-done = bf16[128,4096]{1,0:T(8,128)(2,1)} async-done(((bf16[8,4096]{1,0:T(8,128)(2,1)}), bf16[128,4096]{1,0:T(8,128)(2,1)}) %all-gather.5.cloned.1.call-update) | async-done | bytes 1048592 | tf_op jit(solution)/shard_map/all_gather | solution.py:18
  81.3 8.5 %fusion = bf16[4096,1792]{0,1:T(8,128)(2,1)} fusion(bf16[128,4096]{1,0:T(8,128)(2,1)} %all-gather.5.cloned.1.call-done, bf16[128,896]{1,0:T(8,128)(2,1)S(1)} %get-tuple-element.9, bf16[128,896]{1,0:T(8,128)(2,1)S(1)} %get-tuple-element.8), kind=kOutput, calls=%fused_computation.1 | convolution fusion | flops 1894645760 | bytes 16187392 | tf_op jit(solution)/shard_map/dot_general | solution.py:33
  89.8 0.0 reduce-scatter.5.cloned.1.call-update
  89.8 0.0 reduce-scatter.3.cloned.1.call-start
  89.9 98.1 %all-gather.3.cloned.1.call-done = bf16[4096,1792]{1,0:T(8,128)(2,1)} async-done(((bf16[256,1792]{1,0:T(8,128)(2,1)}), bf16[4096,1792]{1,0:T(8,128)(2,1)}) %all-gather.3.cloned.1.call-update) | async-done | bytes 14680080 | tf_op jit(solution)/shard_map/all_gather | solution.py:21
  188.0 11.0 %convolution_convert_fusion = bf16[128,4096]{1,0:T(8,128)(2,1)} fusion(bf16[4096,1792]{1,0:T(8,128)(2,1)} %all-gather.3.cloned.1.call-done, bf16[128,896]{1,0:T(8,128)(2,1)S(1)} %get-tuple-element.9, bf16[128,896]{1,0:T(8,128)(2,1)S(1)} %get-tuple-element.8), kind=kOutput, calls=%fused_computation.2 | convolution fusion | flops 1880489984 | bytes 16187392 | tf_op jit(solution)/shard_map/dot_general | solution.py:19
  199.0 0.0 reduce-scatter.3.cloned.1.call-update
  199.1 131.7 %reduce-scatter.5.cloned.1.call-done = bf16[256,1792]{0,1:T(8,128)(2,1)} async-done(((bf16[4096,1792]{0,1:T(8,128)(2,1)}), bf16[256,1792]{0,1:T(8,128)(2,1)}) %reduce-scatter.5.cloned.1.call-update) | async-done | bytes 917520 | tf_op jit(solution)/shard_map/reduce_scatter | solution.py:31
  330.8 1.2 fusion.12
  332.0 1.0 copy.9
  333.0 1.0 copy.10
  334.0 70.8 %reduce-scatter.3.cloned.1.call-done = bf16[8,4096]{1,0:T(8,128)(2,1)} async-done(((bf16[128,4096]{1,0:T(8,128)(2,1)}), bf16[8,4096]{1,0:T(8,128)(2,1)}) %reduce-scatter.3.cloned.1.call-update) | async-done | bytes 65552 | tf_op jit(solution)/shard_map/reduce_scatter | solution.py:25
Async XLA Ops:
  7.2 74.2 %all-gather.5.cloned.1.call-start = ((), (), s32[]{:S(2)}) async-start(), calls=%async_computation.4 | async-start | bytes 1114112 | tf_op jit(solution)/shard_map/all_gather | solution.py:18
  7.9 180.1 %all-gather.3.cloned.1.call-start = ((), (), s32[]{:S(2)}) async-start(), calls=%async_computation.2 | async-start | bytes 15597568 | tf_op jit(solution)/shard_map/all_gather | solution.py:21
  10.1 320.7 %reduce-scatter.5.cloned.1.call-start = ((), (), s32[]{:S(2)}) async-start(), calls=%async_computation.5 | async-start | bytes 15597568 | tf_op jit(solution)/shard_map/reduce_scatter | solution.py:31
  89.8 314.9 %reduce-scatter.3.cloned.1.call-start = ((), (), s32[]{:S(2)}) async-start(), calls=%async_computation.3 | async-start | bytes 1114112 | tf_op jit(solution)/shard_map/reduce_scatter | solution.py:25
Sparse Core Ops, SparseCore 0:
  9.8 71.5 all-gather.4
  84.1 103.8 all-gather.2
  192.6 138.1 reduce-scatter.4
  333.8 70.9 reduce-scatter.2
where the time goes:
time: 412 us; the launch traced here: 411 us
  waiting for transfers between devices  371 us (90%)
  matrix products  19.5 us (5%)
  between operations  13.8 us (3%)
    reduce_scatter x1, waiting for transfers between devices, body(): lax.psum_scatter((lax.dot_general(features, both_grads, (((0,), (0,)), ((...  132 us
    all_gather x1, waiting for transfers between devices, body(): lax.all_gather(both_weights, 'dp', axis=0, tiled=True)  98.1 us
    reduce_scatter x1, waiting for transfers between devices, body(): lax.psum_scatter(terms.astype(jnp.bfloat16), 'tensor', scatter_dimension=...  70.8 us
    all_gather x1, waiting for transfers between devices, body(): features = lax.all_gather(activations, 'tensor', axis=0, tiled=True)  69.8 us
    dot_general x1, matrix products, body(): lax.dot_general(both_grads, lax.all_gather(both_weights, 'dp', axis=0, ti...  11 us
    dot_general x1, matrix products, body(): lax.dot_general(features, both_grads, (((0,), (0,)), ((), ())), preferred...  8.48 us
  transfers between devices with their start and end apart: 4, of which 4 were waited for; matrix products, arithmetic and copies ran while one was open for 6% of the time, Pallas kernels for 0%

commit v1 on v0

v1 whole, which is shorter than its diff:
```python
import jax
import jax.numpy as jnp
from jax import lax
from jax.sharding import PartitionSpec as P


def body(activations, gate_pre, up_pre, hidden_grad, gate_weight, up_weight):
    n_dp = lax.axis_size("dp")
    n_tensor = lax.axis_size("tensor")
    own_tokens, model = activations.shape
    rows, width = gate_weight.shape
    group_tokens = gate_pre.shape[0]
    gate_value = gate_pre.astype(jnp.float32)
    up_value = up_pre.astype(jnp.float32)
    upstream = hidden_grad.astype(jnp.float32)
    gate_sigmoid = jax.nn.sigmoid(gate_value)
    grad_up = (upstream * gate_value * gate_sigmoid).astype(jnp.bfloat16)
    grad_gate = (
        upstream * up_value * gate_sigmoid * (1.0 + gate_value * (1.0 - gate_sigmoid))
    ).astype(jnp.bfloat16)
    own_grads = jnp.concatenate((grad_gate, grad_up), axis=1)
    both_weights = jnp.concatenate((gate_weight, up_weight), axis=1)
    all_grads = lax.all_gather(own_grads, "dp", axis=0, tiled=False)

    pieces = activations.reshape(own_tokens, n_dp, rows).transpose(1, 0, 2)
    pieces = lax.all_to_all(pieces, "dp", split_axis=0, concat_axis=0, tiled=True)
    features = lax.all_gather(pieces, "tensor", axis=1, tiled=True)

    terms = lax.dot_general(
        all_grads.reshape(n_dp * group_tokens, 2 * width), both_weights,
        (((1,), (1,)), ((), ())), preferred_element_type=jnp.float32,
    ).astype(jnp.bfloat16)
    terms = terms.reshape(n_dp, n_tensor, own_tokens, rows).transpose(1, 0, 2, 3)
    terms = terms.reshape(n_dp * group_tokens, rows)
    summed = lax.psum_scatter(terms, "tensor", scatter_dimension=0, tiled=True)
    summed = summed.reshape(n_dp, own_tokens, rows)
    input_grad = lax.all_to_all(summed, "dp", split_axis=0, concat_axis=0, tiled=True)
    input_grad = input_grad.transpose(1, 0, 2).reshape(own_tokens, model)

    grad_scale = float(group_tokens * n_dp) ** (-0.5)
    weight_grad = (
        lax.dot_general(
            features.reshape(n_dp * group_tokens, rows), all_grads.reshape(n_dp * group_tokens, 2 * width),
            (((0,), (0,)), ((), ())), preferred_element_type=jnp.float32,
        ) * grad_scale
    ).astype(jnp.bfloat16)
    return (input_grad, weight_grad[:, :width], weight_grad[:, width:])


def solution(mesh):
    in_specs = (
        P(("dp", "tensor"), None),
        P("dp", "tensor"),
        P("dp", "tensor"),
        P("dp", "tensor"),
        P("dp", "tensor"),
        P("dp", "tensor"),
    )
    out_specs = (P(("dp", "tensor"), None), P("dp", "tensor"), P("dp", "tensor"))
    return jax.shard_map(body, mesh=mesh, in_specs=in_specs, out_specs=out_specs, check_vma=False)
```

time: 412 us -> 252 us (0.61)
  the two profiles are of different devices: /device:TPU:8 before, /device:TPU:1 now
where the time goes in v1:
time: 252 us
  waiting for transfers between devices  186 us (74%)
  starting transfers between devices  18.8 us (7%)
  blocking collectives  15.9 us (6%)
  between operations  13.8 us (5%)
  matrix products  10.8 us (4%)
  local copies, waits for them, and re-layouts  3.81 us (2%)
    reduce_scatter x1, waiting for transfers between devices, body(): summed = lax.psum_scatter(terms, 'tensor', scatter_dimension=0, tiled=True)  67.4 us
    all_gather x1, waiting for transfers between devices, body(): all_grads = lax.all_gather(own_grads, 'dp', axis=0, tiled=False)  63.7 us
    all_gather x1, waiting for transfers between devices, body(): features = lax.all_gather(pieces, 'tensor', axis=1, tiled=True)  49.9 us
    all_to_all x1, starting transfers between devices, body(): lax.all_to_all(summed, 'dp', split_axis=0, concat_axis=0, tiled=True)  18.7 us
    all_to_all x1, blocking collectives, body(): lax.all_to_all(pieces, 'dp', split_axis=0, concat_axis=0, tiled=True)  15.9 us
    dot_general x1, matrix products, body(): lax.dot_general(features.reshape(n_dp * group_tokens, rows), all_grads.re...  5.42 us
    dot_general x1, matrix products, body(): lax.dot_general(all_grads.reshape(n_dp * group_tokens, 2 * width), both_w...  5.35 us
    all_to_all x1, waiting for transfers between devices, body(): lax.all_to_all(summed, 'dp', split_axis=0, concat_axis=0, tiled=True)  5.32 us
  transfers between devices with their start and end apart: 4, of which 4 were waited for; matrix products, arithmetic and copies ran while one was open for 6% of the time, Pallas kernels for 0%

profile of v1, /device:TPU:1, one launch (start us, length us, event | category | flops | bytes accessed | tf_op | source)
XLA Modules:
  0.0 251.7 jit_solution(12752439864973103844)
XLA Ops:
  7.2 0.0 all-gather.6.cloned.1.call-start
  7.2 1.4 fusion.8
  8.6 0.8 pad_maximum_fusion
  9.4 0.0 all-gather.6.cloned.1.call-update
  9.4 0.0 all-gather.4.cloned.1.call-start
  9.5 15.9 %all_to_all.10 = bf16[16,8,256]{2,1,0:T(8,128)(2,1)} all-to-all(bf16[16,8,256]{2,1,0:T(8,128)(2,1)} %bitcast.28), channel_id=1, replica_groups=mesh['dp'=16,'tensor'=16] {'dp'}, dimensions={0} | all-to-all | bytes 131072 | tf_op jit(solution)/shard_map/all_to_all | solution.py:26
  25.4 0.0 all-gather.4.cloned.1.call-update
  25.4 0.0 reduce-scatter.2.cloned.1.call-start
  25.5 63.7 %all-gather.6.cloned.1.call-done = bf16[2048,1792]{1,0:T(8,128)(2,1)} async-done(((bf16[128,1792]{1,0:T(8,128)(2,1)}), bf16[2048,1792]{1,0:T(8,128)(2,1)}) %all-gather.6.cloned.1.call-update) | async-done | bytes 7340048 | tf_op jit(solution)/shard_map/all_gather | solution.py:23
  89.2 5.3 %convolution_convert_fusion = bf16[2048,256]{1,0:T(8,128)(2,1)S(1)} fusion(bf16[2048,1792]{1,0:T(8,128)(2,1)} %all-gather.6.cloned.1.call-done, bf16[256,896]{1,0:T(8,128)(2,1)} %param.11, bf16[256,896]{1,0:T(8,128)(2,1)} %param.10), kind=kOutput, calls=%fused_computation.2 | convolution fusion | flops 1881407488 | bytes 9306112 | tf_op jit(solution)/shard_map/dot_general | solution.py:29
  94.5 1.2 copy.11
  95.7 0.0 reduce-scatter.2.cloned.1.call-update
  95.7 49.9 %all-gather.4.cloned.1.call-done = bf16[16,128,256]{2,1,0:T(8,128)(2,1)} async-done(((bf16[16,8,256]{2,1,0:T(8,128)(2,1)}), bf16[16,128,256]{2,1,0:T(8,128)(2,1)}) %all-gather.4.cloned.1.call-update) | async-done | bytes 1048592 | tf_op jit(solution)/shard_map/all_gather | solution.py:27
  145.6 5.4 %fusion.2 = bf16[256,1792]{0,1:T(8,128)(2,1)S(1)} fusion(bf16[16,128,1792]{2,1,0:T(8,128)(2,1)} %bitcast.30, bf16[16,128,256]{2,1,0:T(8,128)(2,1)} %all-gather.4.cloned.1.call-done), kind=kOutput, calls=%fused_computation.4 | convolution fusion | flops 1879965696 | bytes 9306112 | tf_op jit(solution)/shard_map/dot_general | solution.py:42
  151.1 67.4 %reduce-scatter.2.cloned.1.call-done = bf16[128,256]{1,0:T(8,128)(2,1)} async-done(((bf16[2048,256]{1,0:T(8,128)(2,1)}), bf16[128,256]{1,0:T(8,128)(2,1)}) %reduce-scatter.2.cloned.1.call-update) | async-done | bytes 65552 | tf_op jit(solution)/shard_map/reduce_scatter | solution.py:35
  218.5 18.7 %all-to-all-start = ((bf16[16,8,256]{2,1,0:T(8,128)(2,1)}), bf16[16,8,256]{2,1,0:T(8,128)(2,1)S(1)}, u32[]{:S(2)}, u32[]{:S(2)}) async-start(bf16[16,8,256]{2,1,0:T(8,128)(2,1)} %bitcast.29), calls=%async_computation.1 | async-start | bytes 131072 | tf_op jit(solution)/shard_map/all_to_all | solution.py:37
  237.2 0.1 fusion.16
  237.2 1.0 copy.14
  238.2 1.0 copy.13
  239.2 5.3 %all-to-all-done = bf16[16,8,256]{2,1,0:T(8,128)(2,1)S(1)} async-done(((bf16[16,8,256]{2,1,0:T(8,128)(2,1)}), bf16[16,8,256]{2,1,0:T(8,128)(2,1)S(1)}, u32[]{:S(2)}, u32[]{:S(2)}) %all-to-all-start) | async-done | bytes 65568 | tf_op jit(solution)/shard_map/all_to_all | solution.py:37
  244.5 0.6 copy.17
Async XLA Ops:
  7.2 82.0 %all-gather.6.cloned.1.call-start = ((), (), s32[]{:S(2)}) async-start(), calls=%async_computation.5 | async-start | bytes 7798784 | tf_op jit(solution)/shard_map/all_gather | solution.py:23
  9.4 136.2 %all-gather.4.cloned.1.call-start = ((), (), s32[]{:S(2)}) async-start(), calls=%async_computation.4 | async-start | bytes 1114112 | tf_op jit(solution)/shard_map/all_gather | solution.py:27
  25.4 193.1 %reduce-scatter.2.cloned.1.call-start = ((), (), s32[]{:S(2)}) async-start(), calls=%async_computation.3 | async-start | bytes 1114112 | tf_op jit(solution)/shard_map/reduce_scatter | solution.py:35
  218.5 26.0 %all-to-all-start = ((bf16[16,8,256]{2,1,0:T(8,128)(2,1)}), bf16[16,8,256]{2,1,0:T(8,128)(2,1)S(1)}, u32[]{:S(2)}, u32[]{:S(2)}) async-start(bf16[16,8,256]{2,1,0:T(8,128)(2,1)} %bitcast.29), calls=%async_computation.1 | async-start | bytes 131072 | tf_op jit(solution)/shard_map/all_to_all | solution.py:37
Sparse Core Ops, SparseCore 0:
  11.3 77.7 all-gather.5
  90.9 54.7 all-gather.3
  148.2 70.2 reduce-scatter.1

commit v2 on v1

v2 whole, which is shorter than its diff:
```python
import functools

import jax
import jax.numpy as jnp
from jax import lax
from jax.experimental import pallas as pl
from jax.experimental.pallas import tpu as pltpu
from jax.sharding import PartitionSpec as P

MESH = pl.DeviceIdType.MESH
BF16, F32 = jnp.bfloat16, jnp.float32
CHUNKS = ((0, 0), (1, 0), (0, 1), (0, 3), (0, 2), (1, 1), (1, 3), (1, 2))
SLOT = {chunk: at for at, chunk in enumerate(CHUNKS)}
PARTS = 4
N_COPIES = 192


def kernel(
    grad_scale,
    act_hbm, gate_hbm, up_hbm, hidden_hbm, wgate_hbm, wup_hbm,
    igrad_ref, ggrad_hbm, ugrad_hbm,
    act, gate, up, hidden, weights, weights_t, grads,
    a_send, a_recv, a_mine, a_other, a_all, a_t, total, out_buf,
    p_send, p_recv, p_own, z_send, z_recv, f_send, f_recv,
    send_sems, recv_sems, local_sems,
):
    dp, tensor = lax.axis_index("dp"), lax.axis_index("tensor")
    x_hi, y, core = dp // 8, (dp // 2) % 4, dp % 2
    z, x_lo = tensor // 2, tensor % 2
    width = gate.shape[1]

    def dp_peer(rx, ry, rc):
        index = (((x_hi + rx) % 2) * 4 + (y + ry) % 4) * 2 + (core + rc) % 2
        return {"dp": index, "tensor": tensor}, index

    def z_peer(to):
        return {"dp": dp, "tensor": to * 2 + x_lo}

    x_peer = {"dp": dp, "tensor": z * 2 + 1 - x_lo}
    opposite = dp_peer(1, 0, 0)[0]
    above, below = dp_peer(0, 1, 0)[0], dp_peer(0, 3, 0)[0]
    twin = dp_peer(0, 0, 1)[0]

    copies = []

    def send(src, dst, peer):
        at = len(copies)
        copy = pltpu.make_async_remote_copy(
            src_ref=src, dst_ref=dst, send_sem=send_sems.at[at], recv_sem=recv_sems.at[at],
            device_id=peer, device_id_type=MESH,
        )
        copy.start()
        copies.append(copy)
        return copy

    local = []

    def load(src, dst):
        copy = pltpu.make_async_copy(src, dst, local_sems.at[len(local)])
        copy.start()
        local.append(copy)
        return copy

    def rows(j):
        return pl.ds(pl.multiple_of(((z // 2 + 1 + j) % PARTS) * 32, 32), 32)

    loads = []
    act_load = load(act_hbm, act)
    for j in range(PARTS):
        loads.append([load(src.at[rows(j)], dst.at[rows(j)]) for src, dst in (
            (gate_hbm, gate), (up_hbm, up), (hidden_hbm, hidden))])
    weight_loads = [load(wgate_hbm, weights.at[0]), load(wup_hbm, weights.at[1])]

    barrier = pltpu.get_barrier_semaphore()
    peers = [dp_peer(rx, ry, rc)[0] for rx, ry in CHUNKS for rc in range(2) if rx or ry or rc]
    peers += [z_peer((z + k) % 8) for k in range(1, 8)] + [x_peer]
    for peer in peers:
        pl.semaphore_signal(barrier, inc=1, device_id=peer, device_id_type=MESH)

    got = {}

    def send_part(chunk, j, peer, to_chunk, to_core=0):
        at = SLOT[chunk], 0, rows(j)
        return send(grads.at[at], grads.at[SLOT[to_chunk], to_core, rows(j)], peer)

    def to_twin(chunk, j):
        got[chunk, 1, j] = send_part(chunk, j, twin, chunk, 1)

    for j in range(PARTS):
        for copy in loads[j]:
            copy.wait()
        gate_value = gate[rows(j), :].astype(F32)
        up_value = up[rows(j), :].astype(F32)
        upstream = hidden[rows(j), :].astype(F32)
        gate_sigmoid = jax.nn.sigmoid(gate_value)
        scaled = upstream * gate_sigmoid
        grads[0, 0, rows(j), 0:width] = (
            scaled * up_value * (1.0 + gate_value * (1.0 - gate_sigmoid))
        ).astype(BF16)
        grads[0, 0, rows(j), width:2 * width] = (scaled * gate_value).astype(BF16)
        if j == 0:
            pl.semaphore_wait(barrier, len(peers))
        got[(1, 0), 0, j] = send_part((0, 0), j, opposite, (1, 0))
        got[(0, 3), 0, j] = send_part((0, 0), j, above, (0, 3))
        got[(0, 1), 0, j] = send_part((0, 0), j, below, (0, 1))
        to_twin((0, 0), j)

    act_load.wait()
    wide = act[...].astype(F32)
    for index in range(16):
        at = index * 256
        a_send[index] = jnp.concatenate(
            (wide[:, at:at + 128], wide[:, at + 128:at + 256]), axis=0
        ).astype(BF16)
    a_copies = []
    for rx, ry in CHUNKS:
        for rc in range(2):
            if rx or ry or rc:
                peer, index = dp_peer(rx, ry, rc)
                a_copies.append(send(a_send.at[index], a_recv.at[SLOT[rx, -ry % 4], rc], peer))
    a_recv[0, 0] = a_send[dp]

    for copy in weight_loads:
        copy.wait()
    for half in range(2):
        weights_t[half] = weights[half].astype(F32).T.astype(BF16)

    groups = {}

    def wait_parts(chunks, parts, cores=(0, 1)):
        for chunk in chunks:
            for j in parts:
                for rc in cores:
                    if (chunk, rc, j) in got:
                        got.pop((chunk, rc, j)).wait_recv()

    def ig_product(name, chunks, parts):
        first, n = SLOT[chunks[0]], len(chunks)
        base = ig_product.used
        ig_product.used += n * len(parts)
        for at, chunk in enumerate(chunks):
            lhs = jnp.concatenate(
                [grads[SLOT[chunk], rc, rows(j), :] for j in parts for rc in range(2)], axis=0
            )
            term = jnp.dot(lhs[:, :width], weights_t[0], preferred_element_type=F32)
            term += jnp.dot(lhs[:, width:], weights_t[1], preferred_element_type=F32)
            term = term.reshape(len(parts), 2, 2, 2, 8, 256)
            low, high = term[:, :, :, 0], term[:, :, :, 1]
            own = jnp.where(x_lo == 0, low, high)
            other = jnp.where(x_lo == 0, high, low)
            for i in range(len(parts)):
                unit = base + at * len(parts) + i
                for e in range(2):
                    p_own[unit, e] = jnp.concatenate((own[i, 0, e], own[i, 1, e]), axis=0)
                    p_send[unit, e] = jnp.concatenate((other[i, 0, e], other[i, 1, e]), axis=0).astype(BF16)
        units = pl.ds(base, n * len(parts))
        groups[name] = (send(p_send.at[units], p_recv.at[units], x_peer), chunks, parts, base)

    ig_product.used = 0
    z_copies = {}

    def ig_pair(name):
        copy, chunks, parts, base = groups.pop(name)
        first, n = SLOT[chunks[0]], len(chunks)
        copy.wait_recv()
        for at in range(n):
            for i, j in enumerate(parts):
                unit = base + at * len(parts) + i
                z_send[j, :, first + at] = (p_own[unit] + p_recv[unit].astype(F32)).astype(BF16)
        for j in parts:
            for r in range(2):
                if j == PARTS - 1 and r == 0:
                    continue
                e = (z + r) % 2
                to = ((z // 2 + 1 + j) % 4) * 2 + e
                z_copies.setdefault(chunks, []).append(send(
                    z_send.at[j, e, pl.ds(first, n)], z_recv.at[j, r, pl.ds(first, n)], z_peer(to)))

    f_copies = []

    def ig_final(chunks):
        first, n = SLOT[chunks[0]], len(chunks)
        for copy in z_copies.pop(chunks):
            copy.wait_recv()
        for at, (rx, ry) in enumerate(chunks):
            total_z = z_send[PARTS - 1, z % 2, first + at].astype(F32)
            for j in range(PARTS):
                for r in range(2):
                    if j < PARTS - 1 or r:
                        total_z += z_recv[j, r, first + at].astype(F32)
            back = rx * 4 + -ry % 4
            for rc in range(2):
                if rx or ry or rc:
                    f_send[first + at, rc] = total_z[rc * 8:rc * 8 + 8]
                    f_copies.append(send(f_send.at[first + at, rc], f_recv.at[back, rc], dp_peer(rx, ry, rc)[0]))
                else:
                    f_recv[0, 0] = total_z[0:8]

    wait_parts([(0, 0)], range(PARTS))
    ig_product("own", ((0, 0),), range(PARTS))

    for copy in a_copies:
        copy.wait_recv()
    pieces = a_recv[...].astype(F32).reshape(16, 2, 8, 128)
    pieces = jnp.concatenate((pieces[:, 0], pieces[:, 1]), axis=-1)
    a_mine[...] = pieces.reshape(128, 256).astype(BF16)
    a_pair = send(a_mine, a_other, x_peer)

    def forward_own_row(j):
        wait_parts([(1, 0)], [j], (0,))
        got[(1, 3), 0, j] = send_part((1, 0), j, above, (1, 3))
        got[(1, 1), 0, j] = send_part((1, 0), j, below, (1, 1))
        to_twin((1, 0), j)
        wait_parts([(0, 3), (0, 1)], [j], (0,))
        if j % 2 == 0:
            got[(0, 2), 0, j] = send_part((0, 3), j, above, (0, 2))
        else:
            got[(0, 2), 0, j] = send_part((0, 1), j, below, (0, 2))
        to_twin((0, 3), j)
        to_twin((0, 1), j)

    ring = {}

    def ring_step(step):
        right, left = z_peer((z + 1) % 8), z_peer((z + 7) % 8)
        if step:
            ring["right"].wait_recv()
            ring["left"].wait_recv()
        up_block, down_block = (z + 8 - step) % 8, (z + step) % 8
        if step < 3:
            ring["right"] = send(a_all.at[up_block], a_all.at[up_block], right)
            ring["left"] = send(a_all.at[down_block], a_all.at[down_block], left)
        elif step == 3:
            ring["right"] = send(a_all.at[up_block, pl.ds(0, 4)], a_all.at[up_block, pl.ds(0, 4)], right)
            ring["left"] = send(a_all.at[down_block, pl.ds(4, 4)], a_all.at[down_block, pl.ds(4, 4)], left)

    forward_own_row(0)
    a_pair.wait_recv()
    mine = a_mine[...].astype(F32).reshape(16, 8, 256)
    other = a_other[...].astype(F32).reshape(16, 8, 256)
    both = jnp.stack((jnp.where(x_lo == 0, mine, other), jnp.where(x_lo == 0, other, mine)), axis=1)
    a_all[z] = both.reshape(8, 2, 16, 256).astype(BF16)
    ring_step(0)
    ig_pair("own")
    forward_own_row(1)
    ring_step(1)
    forward_own_row(2)
    ring_step(2)
    forward_own_row(3)

    early = ((1, 0), (0, 1), (0, 3))
    wait_parts(early, range(PARTS))
    ig_product("early", early, range(PARTS))
    ring_step(3)
    ig_final(((0, 0),))
    for j in range(PARTS):
        wait_parts([(0, 2)], [j], (0,))
        to_twin((0, 2), j)
    ig_pair("early")

    def forward_other_row(j):
        wait_parts([(1, 3), (1, 1)], [j], (0,))
        if j % 2 == 0:
            got[(1, 2), 0, j] = send_part((1, 3), j, above, (1, 2))
        else:
            got[(1, 2), 0, j] = send_part((1, 1), j, below, (1, 2))
        to_twin((1, 3), j)
        to_twin((1, 1), j)

    forward_other_row(0)
    wait_parts([(0, 2)], range(PARTS))
    ig_product("across", ((0, 2),), range(PARTS))
    ring_step(4)
    for at in range(8):
        block = jnp.concatenate([a_all[zz, at, rc] for rc in range(2) for zz in range(8)], axis=0)
        a_t[:, at * 256:(at + 1) * 256] = block.astype(F32).T.astype(BF16)
    forward_other_row(1)
    late = ((1, 1), (1, 3))
    wait_parts(late, (0, 1))
    ig_product("late0", late, (0, 1))
    ig_pair("across")
    ig_final(early)
    for half in range(2):
        cols = slice(half * width, (half + 1) * width)
        total[:, cols] = jnp.dot(
            a_t[:, 0:1280], grads[0:5, :, :, cols].reshape(1280, width), preferred_element_type=F32)
    forward_other_row(2)
    forward_other_row(3)
    ig_pair("late0")
    wait_parts(late, (2, 3))
    ig_product("late1", late, (2, 3))
    ig_final(((0, 2),))
    for j in range(PARTS):
        wait_parts([(1, 2)], [j], (0,))
        to_twin((1, 2), j)
    ig_pair("late1")
    wait_parts([(1, 2)], range(PARTS))
    ig_product("last", ((1, 2),), range(PARTS))
    outs = []
    for half, out_hbm in enumerate((ggrad_hbm, ugrad_hbm)):
        cols = slice(half * width, (half + 1) * width)
        out_buf[half] = ((total[:, cols] + jnp.dot(
            a_t[:, 1280:2048], grads[5:8, :, :, cols].reshape(768, width), preferred_element_type=F32)
        ) * grad_scale).astype(BF16)
        outs.append(load(out_buf.at[half], out_hbm))
        if half == 0:
            ig_pair("last")
    ig_final(late)
    ig_final(((1, 2),))
    for copy in f_copies:
        copy.wait_recv()
    for index in range(16):
        rel = ((index // 8 + x_hi) % 2) * 4 + (index // 2 % 4 - y + 4) % 4
        igrad_ref[:, index * 256:(index + 1) * 256] = f_recv[rel, (index % 2 + core) % 2].astype(BF16)
    for copy in outs:
        copy.wait()
    for copy in copies:
        copy.wait_send()


def body(*args):
    activations, gate_pre, _, _, gate_weight, _ = args
    own_tokens, model = activations.shape
    rows, width = gate_weight.shape
    tokens = gate_pre.shape[0]
    n_dp = lax.axis_size("dp")
    any_spec = pl.BlockSpec(memory_space=pl.ANY)
    return pl.pallas_call(
        functools.partial(kernel, float(tokens * n_dp) ** (-0.5)),
        out_shape=(
            jax.ShapeDtypeStruct((own_tokens, model), BF16),
            jax.ShapeDtypeStruct((rows, width), BF16),
            jax.ShapeDtypeStruct((rows, width), BF16),
        ),
        in_specs=[any_spec] * 6,
        out_specs=(pl.BlockSpec(memory_space=pltpu.VMEM), any_spec, any_spec),
        scratch_shapes=[
            pltpu.VMEM((own_tokens, model), BF16),
            pltpu.VMEM((tokens, width), BF16),
            pltpu.VMEM((tokens, width), BF16),
            pltpu.VMEM((tokens, width), BF16),
            pltpu.VMEM((2, rows, width), BF16),
            pltpu.VMEM((2, width, rows), BF16),
            pltpu.VMEM((8, 2, tokens, 2 * width), BF16),
            pltpu.VMEM((16, 16, 128), BF16),
            pltpu.VMEM((8, 2, 16, 128), BF16),
            pltpu.VMEM((128, 256), BF16),
            pltpu.VMEM((128, 256), BF16),
            pltpu.VMEM((8, 8, 2, 16, 256), BF16),
            pltpu.VMEM((rows, tokens * n_dp), BF16),
            pltpu.VMEM((rows, 2 * width), F32),
            pltpu.VMEM((2, rows, width), BF16),
            pltpu.VMEM((32, 2, 16, 256), BF16),
            pltpu.VMEM((32, 2, 16, 256), BF16),
            pltpu.VMEM((32, 2, 16, 256), F32),
            pltpu.VMEM((PARTS, 2, 8, 16, 256), BF16),
            pltpu.VMEM((PARTS, 2, 8, 16, 256), BF16),
            pltpu.VMEM((8, 2, 8, 256), F32),
            pltpu.VMEM((8, 2, 8, 256), F32),
            pltpu.SemaphoreType.DMA((N_COPIES,)),
            pltpu.SemaphoreType.DMA((N_COPIES,)),
            pltpu.SemaphoreType.DMA((32,)),
        ],
        compiler_params=pltpu.CompilerParams(
            collective_id=0, has_side_effects=True, vmem_limit_bytes=48 * 2**20
        ),
        cost_estimate=pl.CostEstimate(flops=3_758_096_384, bytes_accessed=4_500_000, transcendentals=114_688),
    )(*args)


def solution(mesh):
    in_specs = (
        P(("dp", "tensor"), None),
        P("dp", "tensor"),
        P("dp", "tensor"),
        P("dp", "tensor"),
        P("dp", "tensor"),
        P("dp", "tensor"),
    )
    out_specs = (P(("dp", "tensor"), None), P("dp", "tensor"), P("dp", "tensor"))
    return jax.shard_map(body, mesh=mesh, in_specs=in_specs, out_specs=out_specs, check_vma=False)
```

time: 252 us -> 88.7 us (0.35)
  waiting for transfers between devices: 186 us -> 0 us
  Pallas kernels: 0 us -> 79.9 us
  starting transfers between devices: 18.8 us -> 0 us
  blocking collectives: 15.9 us -> 0 us
  between operations: 13.8 us -> 0.65 us
  matrix products: 10.8 us -> 0 us
  local copies, waits for them, and re-layouts: 3.81 us -> 7.85 us
    all_gather x2 -> x0, waiting for transfers between devices: 114 us -> none  [the longest x1 63.7 us: body(): all_grads = lax.all_gather(own_grads, 'dp', axis=0, tiled=False)]
    pallas_call x0 -> x1, Pallas kernels: none -> 79.9 us  [body(): pl.pallas_call(functools.partial(kernel, float(tokens * n_dp) ** (-0.5)),...]
    reduce_scatter x1 -> x0, waiting for transfers between devices: 67.4 us -> none  [body(): summed = lax.psum_scatter(terms, 'tensor', scatter_dimension=0, tiled=True)]
    all_to_all x1 -> x0, starting transfers between devices: 18.7 us -> none  [body(): lax.all_to_all(summed, 'dp', split_axis=0, concat_axis=0, tiled=True)]
    all_to_all x1 -> x0, blocking collectives: 15.9 us -> none  [body(): lax.all_to_all(pieces, 'dp', split_axis=0, concat_axis=0, tiled=True)]
    dot_general x2 -> x0, matrix products: 10.8 us -> none  [the longest x1 5.42 us: body(): lax.dot_general(features.reshape(n_dp * group_tokens, rows), all_grads.re...]
    all_to_all x1 -> x0, waiting for transfers between devices: 5.32 us -> none  [body(): lax.all_to_all(summed, 'dp', split_axis=0, concat_axis=0, tiled=True)]
    unnamed x3 -> x15, local copies, waits for them, and re-layouts: 2.58 us -> 7.85 us
  transfers between devices with their start and end apart: 4 -> 0, of which waited for: 4 -> 0; matrix products, arithmetic and copies ran while one was open for 6% -> 0% of each run, Pallas kernels for 0% -> 0%
where the time goes in v2:
time: 88.7 us; the launch traced here: 88.4 us
  Pallas kernels  79.9 us (90%)
  local copies, waits for them, and re-layouts  7.85 us (9%)
    pallas_call x1, Pallas kernels, body(): pl.pallas_call(functools.partial(kernel, float(tokens * n_dp) ** (-0.5)),...  79.9 us
    unnamed x15, local copies, waits for them, and re-layouts  7.85 us

profile of v2, /device:TPU:1, one launch (start us, length us, event | category | flops | bytes accessed | tf_op | source)
XLA Modules:
  0.0 88.4 jit_solution(10255173984056013105)
XLA Ops:
  0.6 0.0 copy-start
  0.6 1.0 %copy-done = bf16[256,896]{1,0:T(8,128)(2,1)S(1)} copy-done((bf16[256,896]{1,0:T(8,128)(2,1)S(1)}, bf16[256,896]{1,0:T(8,128)(2,1)}, u32[]{:S(2)}) %copy-start) | copy-done | bytes 458776
  1.7 0.0 copy-start.1
  1.7 1.0 %copy-done.1 = bf16[256,896]{1,0:T(8,128)(2,1)S(1)} copy-done((bf16[256,896]{1,0:T(8,128)(2,1)S(1)}, bf16[256,896]{1,0:T(8,128)(2,1)}, u32[]{:S(2)}) %copy-start.1) | copy-done | bytes 458776
  2.7 0.0 copy-start.2
  2.7 0.9 %copy-done.2 = bf16[128,896]{1,0:T(8,128)(2,1)S(1)} copy-done((bf16[128,896]{1,0:T(8,128)(2,1)S(1)}, bf16[128,896]{1,0:T(8,128)(2,1)}, u32[]{:S(2)}) %copy-start.2) | copy-done | bytes 229400
  3.6 0.0 copy-start.3
  3.6 0.9 %copy-done.3 = bf16[128,896]{1,0:T(8,128)(2,1)S(1)} copy-done((bf16[128,896]{1,0:T(8,128)(2,1)S(1)}, bf16[128,896]{1,0:T(8,128)(2,1)}, u32[]{:S(2)}) %copy-start.3) | copy-done | bytes 229400
  4.5 0.0 copy-start.4
  4.6 0.9 %copy-done.4 = bf16[128,896]{1,0:T(8,128)(2,1)S(1)} copy-done((bf16[128,896]{1,0:T(8,128)(2,1)S(1)}, bf16[128,896]{1,0:T(8,128)(2,1)}, u32[]{:S(2)}) %copy-start.4) | copy-done | bytes 229400
  5.5 0.0 copy-start.5
  5.5 0.8 copy-done.5
  6.3 79.9 %shard_map.85 = (bf16[8,4096]{1,0:T(8,128)(2,1)S(1)}, bf16[256,896]{1,0:T(8,128)(2,1)S(1)}, bf16[256,896]{1,0:T(8,128)(2,1)S(1)}) custom-call(bf16[8,4096]{1,0:T(8,128)(2,1)S(1)} %copy-done.5, bf16[128,896]{1,0:T(8,128)(2,1)S(1)} %copy-done.2, bf16[128,896]{1,0:T(8,128)(2,1)S(1)} %copy-done.3, bf16[128,896]{1,0:T(8,128)(2,1)S(1)} %copy-done.4, ...), custom_call_target="tpu_custom_call" | custom-call | flops 3758096384 | bytes 4500000 | tf_op jit(solution)/shard_map/pallas_call | solution.py:328
  86.2 0.6 copy.12
  86.9 0.8 copy.13
  87.6 0.8 copy.14
Async XLA Ops:
  0.6 1.0 %copy-start = (bf16[256,896]{1,0:T(8,128)(2,1)S(1)}, bf16[256,896]{1,0:T(8,128)(2,1)}, u32[]{:S(2)}) copy-start(bf16[256,896]{1,0:T(8,128)(2,1)} %wgate_hbm.1) | copy-start | bytes 1376260
  1.7 1.0 %copy-start.1 = (bf16[256,896]{1,0:T(8,128)(2,1)S(1)}, bf16[256,896]{1,0:T(8,128)(2,1)}, u32[]{:S(2)}) copy-start(bf16[256,896]{1,0:T(8,128)(2,1)} %wup_hbm.1) | copy-start | bytes 1376260
  2.7 0.9 %copy-start.2 = (bf16[128,896]{1,0:T(8,128)(2,1)S(1)}, bf16[128,896]{1,0:T(8,128)(2,1)}, u32[]{:S(2)}) copy-start(bf16[128,896]{1,0:T(8,128)(2,1)} %gate_hbm.1) | copy-start | bytes 688132
  3.6 0.9 %copy-start.3 = (bf16[128,896]{1,0:T(8,128)(2,1)S(1)}, bf16[128,896]{1,0:T(8,128)(2,1)}, u32[]{:S(2)}) copy-start(bf16[128,896]{1,0:T(8,128)(2,1)} %up_hbm.1) | copy-start | bytes 688132
  4.5 0.9 %copy-start.4 = (bf16[128,896]{1,0:T(8,128)(2,1)S(1)}, bf16[128,896]{1,0:T(8,128)(2,1)}, u32[]{:S(2)}) copy-start(bf16[128,896]{1,0:T(8,128)(2,1)} %hidden_hbm.1) | copy-start | bytes 688132
  5.5 0.8 copy-start.5

commit v3 on v2

v3 whole, which is shorter than its diff:
```python
import functools

import jax
import jax.numpy as jnp
from jax import lax
from jax.experimental import pallas as pl
from jax.experimental.pallas import tpu as pltpu
from jax.sharding import PartitionSpec as P

MESH = pl.DeviceIdType.MESH
BF16, F32 = jnp.bfloat16, jnp.float32
CHUNKS = ((0, 0), (1, 0), (0, 1), (0, 3), (0, 2), (1, 1), (1, 3), (1, 2))
SLOT = {chunk: at for at, chunk in enumerate(CHUNKS)}
PARTS = 4
N_COPIES = 96


def kernel(
    grad_scale,
    act_hbm, gate_hbm, up_hbm, hidden_hbm, wgate_hbm, wup_hbm,
    igrad_ref, ggrad_ref, ugrad_ref,
    act, gate, up, hidden, weights, weights_t, grads,
    a_send, a_got, a_all, a_t, total,
    p_send, p_recv, p_own, p_out, z_send, z_recv, f_send, f_recv,
    send_sems, recv_sems, local_sems,
):
    dp, tensor = lax.axis_index("dp"), lax.axis_index("tensor")
    x_hi, y, core = dp // 8, (dp // 2) % 4, dp % 2
    z, x_lo = tensor // 2, tensor % 2
    width = gate.shape[1]

    def dp_peer(rx, ry, rc):
        index = (((x_hi + rx) % 2) * 4 + (y + ry) % 4) * 2 + (core + rc) % 2
        return {"dp": index, "tensor": tensor}, index

    def z_peer(to):
        return {"dp": dp, "tensor": to * 2 + x_lo}

    x_peer = {"dp": dp, "tensor": z * 2 + 1 - x_lo}
    opposite = dp_peer(1, 0, 0)[0]
    above, below = dp_peer(0, 1, 0)[0], dp_peer(0, 3, 0)[0]
    twin = dp_peer(0, 0, 1)[0]

    copies = []

    def send(src, dst, peer):
        at = len(copies)
        copy = pltpu.make_async_remote_copy(
            src_ref=src, dst_ref=dst, send_sem=send_sems.at[at], recv_sem=recv_sems.at[at],
            device_id=peer, device_id_type=MESH,
        )
        copy.start()
        copies.append(copy)
        return copy

    local = []

    def load(src, dst):
        copy = pltpu.make_async_copy(src, dst, local_sems.at[len(local)])
        copy.start()
        local.append(copy)
        return copy

    def rows(j):
        return pl.ds(pl.multiple_of(((z // 2 + 1 + j) % PARTS) * 32, 32), 32)

    loads = []
    act_load = load(act_hbm, act.at[0])
    for j in range(PARTS):
        loads.append([load(src.at[rows(j)], dst.at[rows(j)]) for src, dst in (
            (gate_hbm, gate), (up_hbm, up), (hidden_hbm, hidden))])
    weight_loads = [load(wgate_hbm, weights.at[0]), load(wup_hbm, weights.at[1])]

    barrier = pltpu.get_barrier_semaphore()
    peers = [dp_peer(rx, ry, 0)[0] for rx, ry in CHUNKS[1:]] + [twin]
    peers += [z_peer((z + k) % 8) for k in range(1, 8)] + [x_peer]
    for peer in peers:
        pl.semaphore_signal(barrier, inc=1, device_id=peer, device_id_type=MESH)

    got = {}
    a_pairs = []

    def send_part(chunk, j, peer, to_chunk):
        at = rows(j)
        got[to_chunk, j] = send(grads.at[SLOT[chunk], 0, at], grads.at[SLOT[to_chunk], 0, at], peer)

    def to_twin(chunk):
        got["twin", chunk] = send(grads.at[SLOT[chunk], 0], grads.at[SLOT[chunk], 1], twin)

    def wait_parts(chunks, parts):
        for chunk in chunks:
            for j in parts:
                if (chunk, j) in got:
                    got.pop((chunk, j)).wait_recv()

    def own_part(j):
        for copy in loads[j]:
            copy.wait()
        gate_value = gate[rows(j), :].astype(F32)
        up_value = up[rows(j), :].astype(F32)
        upstream = hidden[rows(j), :].astype(F32)
        gate_sigmoid = jax.nn.sigmoid(gate_value)
        scaled = upstream * gate_sigmoid
        grads[0, 0, rows(j), 0:width] = (
            scaled * up_value * (1.0 + gate_value * (1.0 - gate_sigmoid))
        ).astype(BF16)
        grads[0, 0, rows(j), width:2 * width] = (scaled * gate_value).astype(BF16)
        if j == 0:
            pl.semaphore_wait(barrier, len(peers))
            act_load.wait()
            a_pairs.append(send(act.at[0], act.at[1], x_peer))
        send_part((0, 0), j, above, (0, 3))
        send_part((0, 0), j, below, (0, 1))
        send_part((0, 0), j, opposite, (1, 0))

    own_part(0)
    own_part(1)
    a_pairs[0].wait_recv()
    mine, other = act[0].astype(F32), act[1].astype(F32)
    both = jnp.concatenate((jnp.where(x_lo == 0, mine, other), jnp.where(x_lo == 0, other, mine)), axis=0)
    for chip in range(8):
        for rc in range(2):
            at = (chip * 2 + rc) * 256
            a_send[chip, (rc + core) % 2] = both[:, at:at + 256].astype(BF16)
    a_copies = []
    for rx, ry in CHUNKS[1:]:
        peer, index = dp_peer(rx, ry, 0)
        a_copies.append(send(a_send.at[index // 2], a_got.at[SLOT[rx, -ry % 4]], peer))
    a_got[0] = a_send[dp // 2]
    for j in range(2, PARTS):
        own_part(j)
    to_twin((0, 0))
    for copy in weight_loads:
        copy.wait()
    for half in range(2):
        weights_t[0, half] = weights[half].astype(F32).T.astype(BF16)
    w_copy = send(weights_t.at[0], weights_t.at[1], twin)

    def ig_product(units, base):
        for first in range(0, len(units), 8):
            some = units[first:first + 8]
            wait_parts_of(some)
            lhs = jnp.concatenate([grads[SLOT[chunk], 0, rows(j), :] for chunk, j in some], axis=0)
            at = pl.ds(base + first, len(some))
            for rc in range(2):
                term = jnp.dot(lhs[:, :width], weights_t[rc, 0], preferred_element_type=F32)
                term += jnp.dot(lhs[:, width:], weights_t[rc, 1], preferred_element_type=F32)
                term = term.reshape(len(some), 2, 2, 8, 256)
                low, high = term[:, :, 0], term[:, :, 1]
                here = at, slice(None), pl.ds(rc * 8, 8)
                p_own[here] = jnp.where(x_lo == 0, low, high)
                p_out[here] = jnp.where(x_lo == 0, high, low)
            p_send[at] = p_out[at].astype(BF16)

    def wait_parts_of(units):
        for chunk, j in units:
            wait_parts([chunk], [j])

    def ig_exchange(base, n):
        at = pl.ds(base, n)
        return send(p_send.at[at], p_recv.at[at], x_peer)

    z_copies = {}

    def ig_pair(copy, units, base, spans):
        copy.wait_recv()
        for at, (chunk, j) in enumerate(units):
            z_send[j, :, SLOT[chunk]] = (p_own[base + at] + p_recv[base + at].astype(F32)).astype(BF16)
        for first, n, parts in spans:
            for j in parts:
                for r in range(2):
                    if j == PARTS - 1 and r == 0:
                        continue
                    e = (z + r) % 2
                    to = ((z // 2 + 1 + j) % 4) * 2 + e
                    at = pl.ds(first, n)
                    z_copies.setdefault(first, []).append(
                        send(z_send.at[j, e, at], z_recv.at[j, r, at], z_peer(to)))

    f_copies = []

    def ig_final(chunks):
        first = SLOT[chunks[0]]
        for copy in z_copies.pop(first):
            copy.wait_recv()
        for at, (rx, ry) in enumerate(chunks):
            total_z = z_send[PARTS - 1, z % 2, first + at].astype(F32)
            for j in range(PARTS):
                for r in range(2):
                    if j < PARTS - 1 or r:
                        total_z += z_recv[j, r, first + at].astype(F32)
            if rx or ry:
                f_send[first + at] = total_z
                back = rx * 4 + -ry % 4
                f_copies.append(send(f_send.at[first + at], f_recv.at[back], dp_peer(rx, ry, 0)[0]))
            else:
                f_recv[0] = total_z

    every = range(PARTS)

    def own_row(j):
        wait_parts([(0, 3), (0, 1)], [j])
        if j % 2 == 0:
            send_part((0, 3), j, above, (0, 2))
        wait_parts([(1, 0)], [j])
        send_part((1, 0), j, above, (1, 3))
        send_part((1, 0), j, below, (1, 1))
        if j % 2 == 1:
            send_part((0, 1), j, below, (0, 2))

    ring = {}

    def ring_step(step):
        right, left = z_peer((z + 1) % 8), z_peer((z + 7) % 8)
        if step:
            ring["right"].wait_recv()
            ring["left"].wait_recv()
        else:
            a_twin.wait_recv()
        up_block, down_block = (z + 8 - step) % 8, (z + step) % 8
        if step < 3:
            ring["right"] = send(a_all.at[up_block], a_all.at[up_block], right)
            ring["left"] = send(a_all.at[down_block], a_all.at[down_block], left)
        elif step == 3:
            ring["right"] = send(a_all.at[up_block, pl.ds(0, 4)], a_all.at[up_block, pl.ds(0, 4)], right)
            ring["left"] = send(a_all.at[down_block, pl.ds(4, 4)], a_all.at[down_block, pl.ds(4, 4)], left)

    def a_turn(at):
        block = jnp.concatenate([a_all[zz, at, rc] for rc in range(2) for zz in range(8)], axis=0)
        a_t[:, at * 256:(at + 1) * 256] = block.astype(F32).T.astype(BF16)

    sent = [0]

    def drain():
        for copy in copies[sent[0]:]:
            copy.wait_send()
        sent[0] = len(copies)

    own_row(0)
    w_copy.wait_recv()
    for copy in a_copies:
        copy.wait_recv()
    a_all[z, :, 0] = a_got[:, 0]
    a_twin = send(a_got.at[:, 1], a_all.at[z, :, 1], twin)
    own_row(1)
    near = [(chunk, j) for chunk in CHUNKS[:4] for j in every]
    ig_product(near[:4], 0)
    own_row(2)
    ring_step(0)
    own_row(3)
    for chunk in CHUNKS[1:4]:
        to_twin(chunk)
    ig_product(near[4:], 4)
    near_copy = ig_exchange(0, 16)
    ring_step(1)
    for j in range(2):
        wait_parts([(0, 2)], [j])
        send_part((0, 2), j, opposite, (1, 2))
    ig_pair(near_copy, near, 0, [(0, 4, every)])
    middle = [(chunk, j) for chunk in CHUNKS[4:7] for j in range(2)]
    ig_product(middle, 16)
    middle_copy = ig_exchange(16, 6)
    ring_step(2)
    wait_parts([(1, 3)], [2])
    send_part((1, 3), 2, above, (1, 2))
    ring_step(3)
    ig_pair(middle_copy, middle, 16, [(4, 3, range(2))])
    wait_parts([(1, 1)], [3])
    send_part((1, 1), 3, below, (1, 2))
    wait_parts(CHUNKS[4:7], every)
    for chunk in CHUNKS[4:7]:
        to_twin(chunk)
    far = [(chunk, j) for chunk in CHUNKS[4:7] for j in range(2, 4)] + [((1, 2), j) for j in range(2)]
    ig_product(far, 22)
    far_copy = ig_exchange(22, 8)
    ig_final(CHUNKS[:4])
    ring_step(4)
    for at in range(8):
        a_turn(at)
    last = [((1, 2), j) for j in range(2, 4)]
    ig_product(last, 30)
    last_copy = ig_exchange(30, 2)
    to_twin((1, 2))
    ig_pair(far_copy, far, 22, [(4, 3, range(2, 4)), (7, 1, range(2))])
    for chunk in CHUNKS[:5]:
        got.pop(("twin", chunk)).wait_recv()
    for half in range(2):
        cols = slice(half * width, (half + 1) * width)
        total[:, cols] = jnp.dot(
            a_t[:, 0:1280], grads[0:5, :, :, cols].reshape(1280, width), preferred_element_type=F32)
    ig_pair(last_copy, last, 30, [(7, 1, range(2, 4))])
    ig_final(CHUNKS[4:7])
    for chunk in CHUNKS[5:]:
        got.pop(("twin", chunk)).wait_recv()
    for half, out_ref in enumerate((ggrad_ref, ugrad_ref)):
        cols = slice(half * width, (half + 1) * width)
        out_ref[...] = ((total[:, cols] + jnp.dot(
            a_t[:, 1280:2048], grads[5:8, :, :, cols].reshape(768, width), preferred_element_type=F32)
        ) * grad_scale).astype(BF16)
        if half == 0:
            ig_final(CHUNKS[7:])
    drain()
    assert not got
    for copy in f_copies:
        copy.wait_recv()
    for index in range(16):
        rel = ((index // 8 + x_hi) % 2) * 4 + (index // 2 % 4 - y + 4) % 4
        at = pl.ds(pl.multiple_of(((index % 2 + core) % 2) * 8, 8), 8)
        igrad_ref[:, index * 256:(index + 1) * 256] = f_recv[rel, at].astype(BF16)


def body(*args):
    activations, gate_pre, _, _, gate_weight, _ = args
    own_tokens, model = activations.shape
    rows, width = gate_weight.shape
    tokens = gate_pre.shape[0]
    n_dp = lax.axis_size("dp")
    hbm, vmem = pl.BlockSpec(memory_space=pltpu.HBM), pl.BlockSpec(memory_space=pltpu.VMEM)
    results = pl.pallas_call(
        functools.partial(kernel, float(tokens * n_dp) ** (-0.5)),
        out_shape=(
            jax.ShapeDtypeStruct((own_tokens, model), BF16),
            jax.ShapeDtypeStruct((rows, width), BF16),
            jax.ShapeDtypeStruct((rows, width), BF16),
        ),
        in_specs=[hbm] * 6,
        out_specs=(vmem, vmem, vmem),
        scratch_shapes=[
            pltpu.VMEM((2, own_tokens, model), BF16),
            pltpu.VMEM((tokens, width), BF16),
            pltpu.VMEM((tokens, width), BF16),
            pltpu.VMEM((tokens, width), BF16),
            pltpu.VMEM((2, rows, width), BF16),
            pltpu.VMEM((2, 2, width, rows), BF16),
            pltpu.VMEM((8, 2, tokens, 2 * width), BF16),
            pltpu.VMEM((8, 2, 16, 256), BF16),
            pltpu.VMEM((8, 2, 16, 256), BF16),
            pltpu.VMEM((8, 8, 2, 16, 256), BF16),
            pltpu.VMEM((rows, tokens * n_dp), BF16),
            pltpu.VMEM((rows, 2 * width), F32),
            pltpu.VMEM((32, 2, 16, 256), BF16),
            pltpu.VMEM((32, 2, 16, 256), BF16),
            pltpu.VMEM((32, 2, 16, 256), F32),
            pltpu.VMEM((32, 2, 16, 256), F32),
            pltpu.VMEM((PARTS, 2, 8, 16, 256), BF16),
            pltpu.VMEM((PARTS, 2, 8, 16, 256), BF16),
            pltpu.VMEM((8, 16, 256), F32),
            pltpu.VMEM((8, 16, 256), F32),
            pltpu.SemaphoreType.DMA((N_COPIES,)),
            pltpu.SemaphoreType.DMA((N_COPIES,)),
            pltpu.SemaphoreType.DMA((32,)),
        ],
        compiler_params=pltpu.CompilerParams(
            collective_id=0, has_side_effects=True, vmem_limit_bytes=62 * 2**20
        ),
        cost_estimate=pl.CostEstimate(flops=3_758_096_384, bytes_accessed=4_500_000, transcendentals=114_688),
    )(*args)
    return pl.pallas_call(
        place,
        out_shape=tuple(jax.ShapeDtypeStruct(r.shape, r.dtype) for r in results),
        in_specs=[hbm] * 3,
        out_specs=(hbm,) * 3,
        scratch_shapes=[pltpu.VMEM(r.shape, r.dtype) for r in results] + [pltpu.SemaphoreType.DMA((6,))],
    )(*results)


def place(a_in, b_in, c_in, a_out, b_out, c_out, a, b, c, sems):
    steps = ((b_in, b, b_out), (c_in, c, c_out), (a_in, a, a_out))
    copies = [pltpu.make_async_copy(src, mid, sems.at[at]) for at, (src, mid, _) in enumerate(steps)]
    for copy in copies:
        copy.start()
    outs = []
    for at, (_, mid, dst) in enumerate(steps):
        copies[at].wait()
        outs.append(pltpu.make_async_copy(mid, dst, sems.at[3 + at]))
        outs[at].start()
    for copy in outs:
        copy.wait()


def solution(mesh):
    in_specs = (
        P(("dp", "tensor"), None),
        P("dp", "tensor"),
        P("dp", "tensor"),
        P("dp", "tensor"),
        P("dp", "tensor"),
        P("dp", "tensor"),
    )
    out_specs = (P(("dp", "tensor"), None), P("dp", "tensor"), P("dp", "tensor"))
    return jax.shard_map(body, mesh=mesh, in_specs=in_specs, out_specs=out_specs, check_vma=False)
```

time: 88.7 us -> 65.1 us (0.73)
  the two profiles are of different devices: /device:TPU:1 before, /device:TPU:4 now
where the time goes in v3:
time: 65.1 us; the launch traced here: 65 us
  Pallas kernels  64.4 us (99%)
    pallas_call x1, Pallas kernels, body(): pl.pallas_call(functools.partial(kernel, float(tokens * n_dp) ** (-0.5)),...  62.4 us
    pallas_call x1, Pallas kernels, body(): pl.pallas_call(place, out_shape=tuple((jax.ShapeDtypeStruct(r.shape, r.dt...  2 us

profile of v3, /device:TPU:4, one launch (start us, length us, event | category | flops | bytes accessed | tf_op | source)
XLA Modules:
  0.0 65.0 jit_solution(8878061786403551383)
XLA Ops:
  0.6 62.4 %shard_map.85 = (bf16[8,4096]{1,0:T(8,128)(2,1)}, bf16[256,896]{1,0:T(8,128)(2,1)}, bf16[256,896]{1,0:T(8,128)(2,1)}) custom-call(bf16[8,4096]{1,0:T(8,128)(2,1)} %act_hbm.1, bf16[128,896]{1,0:T(8,128)(2,1)} %gate_hbm.1, bf16[128,896]{1,0:T(8,128)(2,1)} %up_hbm.1, bf16[128,896]{1,0:T(8,128)(2,1)} %hidden_hbm.1, bf16[256,896]{1,0:T(8,128)(2,1)} %wgate_hbm.1, ...), custom_call_target="tpu_custom_call" | custom-call | flops 3758096384 | bytes 4500000 | tf_op jit(solution)/shard_map/pallas_call | solution.py:319
  63.0 2.0 %shard_map.86 = (bf16[8,4096]{1,0:T(8,128)(2,1)}, bf16[256,896]{1,0:T(8,128)(2,1)}, bf16[256,896]{1,0:T(8,128)(2,1)}) custom-call(bf16[8,4096]{1,0:T(8,128)(2,1)} %get-tuple-element.6.a_in, bf16[256,896]{1,0:T(8,128)(2,1)} %get-tuple-element.7.b_in, bf16[256,896]{1,0:T(8,128)(2,1)} %get-tuple-element.8.c_in), custom_call_target="tpu_custom_call" | custom-call | tf_op jit(solution)/shard_map/pallas_call | solution.py:358

commit v4 on v3

--- a/solution.py
+++ b/solution.py
@@ -9,18 +9,18 @@
 
 MESH = pl.DeviceIdType.MESH
 BF16, F32 = jnp.bfloat16, jnp.float32
-CHUNKS = ((0, 0), (1, 0), (0, 1), (0, 3), (0, 2), (1, 1), (1, 3), (1, 2))
+CHUNKS = ((0, 0), (1, 0), (0, 2), (1, 1), (1, 3), (1, 2), (0, 1), (0, 3))
 SLOT = {chunk: at for at, chunk in enumerate(CHUNKS)}
 PARTS = 4
-N_COPIES = 96
+N_COPIES = 112
 
 
 def kernel(
     grad_scale,
     act_hbm, gate_hbm, up_hbm, hidden_hbm, wgate_hbm, wup_hbm,
-    igrad_ref, ggrad_ref, ugrad_ref,
+    igrad_hbm, ggrad_hbm, ugrad_hbm,
     act, gate, up, hidden, weights, weights_t, grads,
-    a_send, a_got, a_all, a_t, total,
+    a_send, a_got, a_all, a_t, total, out_buf, igrad,
     p_send, p_recv, p_own, p_out, z_send, z_recv, f_send, f_recv,
     send_sems, recv_sems, local_sems,
 ):
@@ -29,12 +29,22 @@
     z, x_lo = tensor // 2, tensor % 2
     width = gate.shape[1]
 
+    @functools.lru_cache(None)
     def dp_peer(rx, ry, rc):
         index = (((x_hi + rx) % 2) * 4 + (y + ry) % 4) * 2 + (core + rc) % 2
         return {"dp": index, "tensor": tensor}, index
 
     def z_peer(to):
         return {"dp": dp, "tensor": to * 2 + x_lo}
+
+    @functools.lru_cache(None)
+    def part_peer(j, r):
+        pair, e = (z // 2 + 1 + j) % 4, (z + r) % 2
+        return z_peer(pair * 2 + e), e
+
+    @functools.lru_cache(None)
+    def z_at(k):
+        return (z + k) % 8
 
     x_peer = {"dp": dp, "tensor": z * 2 + 1 - x_lo}
     opposite = dp_peer(1, 0, 0)[0]
@@ -61,19 +71,21 @@
         local.append(copy)
         return copy
 
+    @functools.lru_cache(None)
     def rows(j):
         return pl.ds(pl.multiple_of(((z // 2 + 1 + j) % PARTS) * 32, 32), 32)
 
+    act_load = load(act_hbm, act.at[0])
     loads = []
-    act_load = load(act_hbm, act.at[0])
-    for j in range(PARTS):
+
+    def load_part(j):
         loads.append([load(src.at[rows(j)], dst.at[rows(j)]) for src, dst in (
             (gate_hbm, gate), (up_hbm, up), (hidden_hbm, hidden))])
-    weight_loads = [load(wgate_hbm, weights.at[0]), load(wup_hbm, weights.at[1])]
-
+
+    load_part(0)
     barrier = pltpu.get_barrier_semaphore()
     peers = [dp_peer(rx, ry, 0)[0] for rx, ry in CHUNKS[1:]] + [twin]
-    peers += [z_peer((z + k) % 8) for k in range(1, 8)] + [x_peer]
+    peers += [part_peer(j, r)[0] for j in range(PARTS) for r in range(2) if j < PARTS - 1 or r] + [x_peer]
     for peer in peers:
         pl.semaphore_signal(barrier, inc=1, device_id=peer, device_id_type=MESH)
 
@@ -109,12 +121,18 @@
             pl.semaphore_wait(barrier, len(peers))
             act_load.wait()
             a_pairs.append(send(act.at[0], act.at[1], x_peer))
-        send_part((0, 0), j, above, (0, 3))
-        send_part((0, 0), j, below, (0, 1))
+        if j % 2 == 0:
+            send_part((0, 0), j, above, (0, 3))
+        else:
+            send_part((0, 0), j, below, (0, 1))
         send_part((0, 0), j, opposite, (1, 0))
 
     own_part(0)
-    own_part(1)
+    for j in range(1, PARTS):
+        load_part(j)
+    weight_loads = [load(wgate_hbm, weights.at[0]), load(wup_hbm, weights.at[1])]
+    for j in range(1, PARTS):
+        own_part(j)
     a_pairs[0].wait_recv()
     mine, other = act[0].astype(F32), act[1].astype(F32)
     both = jnp.concatenate((jnp.where(x_lo == 0, mine, other), jnp.where(x_lo == 0, other, mine)), axis=0)
@@ -127,8 +145,6 @@
         peer, index = dp_peer(rx, ry, 0)
         a_copies.append(send(a_send.at[index // 2], a_got.at[SLOT[rx, -ry % 4]], peer))
     a_got[0] = a_send[dp // 2]
-    for j in range(2, PARTS):
-        own_part(j)
     to_twin((0, 0))
     for copy in weight_loads:
         copy.wait()
@@ -171,11 +187,10 @@
                 for r in range(2):
                     if j == PARTS - 1 and r == 0:
                         continue
-                    e = (z + r) % 2
-                    to = ((z // 2 + 1 + j) % 4) * 2 + e
+                    peer, e = part_peer(j, r)
                     at = pl.ds(first, n)
-                    z_copies.setdefault(first, []).append(
-                        send(z_send.at[j, e, at], z_recv.at[j, r, at], z_peer(to)))
+                    z_copies.setdefault((0, 0, 2, 2, 2, 5, 6, 6)[first], []).append(
+                        send(z_send.at[j, e, at], z_recv.at[j, r, at], peer))
 
     f_copies = []
 
@@ -198,32 +213,34 @@
 
     every = range(PARTS)
 
-    def own_row(j):
-        wait_parts([(0, 3), (0, 1)], [j])
-        if j % 2 == 0:
-            send_part((0, 3), j, above, (0, 2))
+    def on_even(j):
+        wait_parts([(0, 3)], [j])
+        send_part((0, 3), j, above, (0, 2))
+
+    def on_odd(j):
+        wait_parts([(0, 1)], [j])
+        send_part((0, 1), j, below, (0, 2))
+
+    def opposite_part(j, order):
         wait_parts([(1, 0)], [j])
-        send_part((1, 0), j, above, (1, 3))
-        send_part((1, 0), j, below, (1, 1))
-        if j % 2 == 1:
-            send_part((0, 1), j, below, (0, 2))
+        for peer, to_chunk in order:
+            send_part((1, 0), j, peer, to_chunk)
+
+    up_first = ((above, (1, 3)), (below, (1, 1)))
 
     ring = {}
 
     def ring_step(step):
-        right, left = z_peer((z + 1) % 8), z_peer((z + 7) % 8)
-        if step:
-            ring["right"].wait_recv()
-            ring["left"].wait_recv()
-        else:
+        if step == 0:
             a_twin.wait_recv()
-        up_block, down_block = (z + 8 - step) % 8, (z + step) % 8
-        if step < 3:
-            ring["right"] = send(a_all.at[up_block], a_all.at[up_block], right)
-            ring["left"] = send(a_all.at[down_block], a_all.at[down_block], left)
-        elif step == 3:
-            ring["right"] = send(a_all.at[up_block, pl.ds(0, 4)], a_all.at[up_block, pl.ds(0, 4)], right)
-            ring["left"] = send(a_all.at[down_block, pl.ds(4, 4)], a_all.at[down_block, pl.ds(4, 4)], left)
+        for half in range(2):
+            for way, peer, block in (
+                ("right", z_peer(z_at(1)), z_at(8 - step)), ("left", z_peer(z_at(7)), z_at(step))):
+                if (way, half) in ring:
+                    ring.pop((way, half)).wait_recv()
+                if step < 3 or (step == 3 and half == (way == "left")):
+                    part = a_all.at[block, pl.ds(half * 4, 4)]
+                    ring[way, half] = send(part, part, peer)
 
     def a_turn(at):
         block = jnp.concatenate([a_all[zz, at, rc] for rc in range(2) for zz in range(8)], axis=0)
@@ -236,69 +253,88 @@
             copy.wait_send()
         sent[0] = len(copies)
 
-    own_row(0)
+    on_even(0)
+    on_odd(1)
+    opposite_part(0, up_first)
     w_copy.wait_recv()
+    near = [(CHUNKS[at], j) for at in (0, 1) for j in every] + [((0, 3), 0), ((0, 3), 2), ((0, 1), 1), ((0, 1), 3)]
+    ig_product(near[:4], 0)
+    on_even(2)
+    opposite_part(1, up_first[::-1])
+    on_odd(3)
     for copy in a_copies:
         copy.wait_recv()
     a_all[z, :, 0] = a_got[:, 0]
     a_twin = send(a_got.at[:, 1], a_all.at[z, :, 1], twin)
-    own_row(1)
-    near = [(chunk, j) for chunk in CHUNKS[:4] for j in every]
-    ig_product(near[:4], 0)
-    own_row(2)
+    opposite_part(2, up_first)
     ring_step(0)
-    own_row(3)
-    for chunk in CHUNKS[1:4]:
+    opposite_part(3, up_first)
+    to_twin((1, 0))
+    wait_parts([(1, 3)], [0])
+    send_part((1, 3), 0, above, (1, 2))
+    for j in (1, 3):
+        send_part((0, 0), j, above, (0, 3))
+    ig_product(near[4:], 4)
+    near_copy = ig_exchange(0, 12)
+    wait_parts([(1, 1)], [1])
+    send_part((1, 1), 1, below, (1, 2))
+    for j in (0, 2):
+        send_part((0, 0), j, below, (0, 1))
+    wait_parts([(0, 2)], [2])
+    send_part((0, 2), 2, opposite, (1, 2))
+    ring_step(1)
+    wait_parts([(0, 2)], [3])
+    send_part((0, 2), 3, opposite, (1, 2))
+    middle = [(chunk, j) for chunk in CHUNKS[2:5] for j in range(2)]
+    ig_product(middle, 12)
+    middle_copy = ig_exchange(12, 6)
+    ring_step(2)
+    ig_pair(near_copy, near, 0, [(0, 2, every), (7, 1, (0, 2)), (6, 1, (1, 3))])
+    later = [(chunk, j) for chunk in CHUNKS[2:5] for j in range(2, 4)]
+    ig_product(later, 18)
+    later_copy = ig_exchange(18, 6)
+    for chunk in CHUNKS[2:5]:
         to_twin(chunk)
-    ig_product(near[4:], 4)
-    near_copy = ig_exchange(0, 16)
-    ring_step(1)
-    for j in range(2):
-        wait_parts([(0, 2)], [j])
-        send_part((0, 2), j, opposite, (1, 2))
-    ig_pair(near_copy, near, 0, [(0, 4, every)])
-    middle = [(chunk, j) for chunk in CHUNKS[4:7] for j in range(2)]
-    ig_product(middle, 16)
-    middle_copy = ig_exchange(16, 6)
-    ring_step(2)
-    wait_parts([(1, 3)], [2])
-    send_part((1, 3), 2, above, (1, 2))
+    ig_pair(middle_copy, middle, 12, [(2, 3, range(2))])
     ring_step(3)
-    ig_pair(middle_copy, middle, 16, [(4, 3, range(2))])
-    wait_parts([(1, 1)], [3])
-    send_part((1, 1), 3, below, (1, 2))
-    wait_parts(CHUNKS[4:7], every)
-    for chunk in CHUNKS[4:7]:
-        to_twin(chunk)
-    far = [(chunk, j) for chunk in CHUNKS[4:7] for j in range(2, 4)] + [((1, 2), j) for j in range(2)]
-    ig_product(far, 22)
-    far_copy = ig_exchange(22, 8)
-    ig_final(CHUNKS[:4])
+    across = [((1, 2), j) for j in every]
+    ig_product(across, 24)
+    across_copy = ig_exchange(24, 4)
+    to_twin((1, 2))
+    ig_pair(later_copy, later, 18, [(2, 3, range(2, 4))])
+    ig_final(CHUNKS[:2])
+    far = [((0, 3), 1), ((0, 1), 0)]
+    ig_product(far, 28)
+    far_copy = ig_exchange(28, 2)
+    ig_pair(across_copy, across, 24, [(5, 1, every)])
+    last = [((0, 3), 3), ((0, 1), 2)]
+    ig_product(last, 30)
+    last_copy = ig_exchange(30, 2)
+    to_twin((0, 3))
+    to_twin((0, 1))
+    ig_pair(far_copy, far, 28, [(7, 1, (1,)), (6, 1, (0,))])
     ring_step(4)
     for at in range(8):
         a_turn(at)
-    last = [((1, 2), j) for j in range(2, 4)]
-    ig_product(last, 30)
-    last_copy = ig_exchange(30, 2)
-    to_twin((1, 2))
-    ig_pair(far_copy, far, 22, [(4, 3, range(2, 4)), (7, 1, range(2))])
-    for chunk in CHUNKS[:5]:
+    ig_pair(last_copy, last, 30, [(7, 1, (3,)), (6, 1, (2,))])
+    ig_final(CHUNKS[2:5])
+    ig_final(CHUNKS[5:6])
+    for chunk in CHUNKS[:6]:
         got.pop(("twin", chunk)).wait_recv()
     for half in range(2):
         cols = slice(half * width, (half + 1) * width)
         total[:, cols] = jnp.dot(
-            a_t[:, 0:1280], grads[0:5, :, :, cols].reshape(1280, width), preferred_element_type=F32)
-    ig_pair(last_copy, last, 30, [(7, 1, range(2, 4))])
-    ig_final(CHUNKS[4:7])
-    for chunk in CHUNKS[5:]:
+            a_t[:, 0:1536], grads[0:6, :, :, cols].reshape(1536, width), preferred_element_type=F32)
+    ig_final(CHUNKS[6:])
+    for chunk in CHUNKS[6:]:
         got.pop(("twin", chunk)).wait_recv()
-    for half, out_ref in enumerate((ggrad_ref, ugrad_ref)):
+    outs = []
+    for half, out_hbm in enumerate((ggrad_hbm, ugrad_hbm)):
         cols = slice(half * width, (half + 1) * width)
-        out_ref[...] = ((total[:, cols] + jnp.dot(
-            a_t[:, 1280:2048], grads[5:8, :, :, cols].reshape(768, width), preferred_element_type=F32)
+        out_buf[half] = ((total[:, cols] + jnp.dot(
+            a_t[:, 1536:2048], grads[6:8, :, :, cols].reshape(512, width), preferred_element_type=F32)
         ) * grad_scale).astype(BF16)
-        if half == 0:
-            ig_final(CHUNKS[7:])
+        outs.append(load(out_buf.at[half], out_hbm))
     drain()
     assert not got
     for copy in f_copies:
@@ -306,7 +342,10 @@
     for index in range(16):
         rel = ((index // 8 + x_hi) % 2) * 4 + (index // 2 % 4 - y + 4) % 4
         at = pl.ds(pl.multiple_of(((index % 2 + core) % 2) * 8, 8), 8)
-        igrad_ref[:, index * 256:(index + 1) * 256] = f_recv[rel, at].astype(BF16)
+        igrad[:, index * 256:(index + 1) * 256] = f_recv[rel, at].astype(BF16)
+    outs.append(load(igrad, igrad_hbm))
+    for copy in outs:
+        copy.wait()
 
 
 def body(*args):
@@ -315,7 +354,7 @@
     rows, width = gate_weight.shape
     tokens = gate_pre.shape[0]
     n_dp = lax.axis_size("dp")
-    hbm, vmem = pl.BlockSpec(memory_space=pltpu.HBM), pl.BlockSpec(memory_space=pltpu.VMEM)
+    hbm = pl.BlockSpec(memory_space=pltpu.HBM)
     results = pl.pallas_call(
         functools.partial(kernel, float(tokens * n_dp) ** (-0.5)),
         out_shape=(
@@ -324,7 +363,7 @@
             jax.ShapeDtypeStruct((rows, width), BF16),
         ),
         in_specs=[hbm] * 6,
-        out_specs=(vmem, vmem, vmem),
+        out_specs=(hbm, hbm, hbm),
         scratch_shapes=[
             pltpu.VMEM((2, own_tokens, model), BF16),
             pltpu.VMEM((tokens, width), BF16),
@@ -338,6 +377,8 @@
             pltpu.VMEM((8, 8, 2, 16, 256), BF16),
             pltpu.VMEM((rows, tokens * n_dp), BF16),
             pltpu.VMEM((rows, 2 * width), F32),
+            pltpu.VMEM((2, rows, width), BF16),
+            pltpu.VMEM((own_tokens, model), BF16),
             pltpu.VMEM((32, 2, 16, 256), BF16),
             pltpu.VMEM((32, 2, 16, 256), BF16),
             pltpu.VMEM((32, 2, 16, 256), F32),

time: 65.1 us -> 62.8 us (0.965)
  the two profiles are of different devices: /device:TPU:4 before, /device:TPU:1 now
where the time goes in v4:
time: 62.8 us; the launch traced here: 62.6 us
  Pallas kernels  61.9 us (99%)
  between operations  0.64 us (1%)
    pallas_call x1, Pallas kernels, body(): pl.pallas_call(functools.partial(kernel, float(tokens * n_dp) ** (-0.5)),...  59.9 us
    pallas_call x1, Pallas kernels, body(): pl.pallas_call(place, out_shape=tuple((jax.ShapeDtypeStruct(r.shape, r.dt...  2 us

profile of v4, /device:TPU:1, one launch (start us, length us, event | category | flops | bytes accessed | tf_op | source)
XLA Modules:
  0.0 62.6 jit_solution(529632599378566580)
XLA Ops:
  0.6 59.9 %shard_map.85 = (bf16[8,4096]{1,0:T(8,128)(2,1)}, bf16[256,896]{1,0:T(8,128)(2,1)}, bf16[256,896]{1,0:T(8,128)(2,1)}) custom-call(bf16[8,4096]{1,0:T(8,128)(2,1)} %act_hbm.1, bf16[128,896]{1,0:T(8,128)(2,1)} %gate_hbm.1, bf16[128,896]{1,0:T(8,128)(2,1)} %up_hbm.1, bf16[128,896]{1,0:T(8,128)(2,1)} %hidden_hbm.1, bf16[256,896]{1,0:T(8,128)(2,1)} %wgate_hbm.1, ...), custom_call_target="tpu_custom_call" | custom-call | flops 3758096384 | bytes 4500000 | tf_op jit(solution)/shard_map/pallas_call | solution.py:358
  60.6 2.0 %shard_map.86 = (bf16[8,4096]{1,0:T(8,128)(2,1)}, bf16[256,896]{1,0:T(8,128)(2,1)}, bf16[256,896]{1,0:T(8,128)(2,1)}) custom-call(bf16[8,4096]{1,0:T(8,128)(2,1)} %get-tuple-element.6.a_in, bf16[256,896]{1,0:T(8,128)(2,1)} %get-tuple-element.7.b_in, bf16[256,896]{1,0:T(8,128)(2,1)} %get-tuple-element.8.c_in), custom_call_target="tpu_custom_call" | custom-call | tf_op jit(solution)/shard_map/pallas_call | solution.py:399

commit v5 on v4

--- a/solution.py
+++ b/solution.py
@@ -319,13 +319,13 @@
     ig_pair(last_copy, last, 30, [(7, 1, (3,)), (6, 1, (2,))])
     ig_final(CHUNKS[2:5])
     ig_final(CHUNKS[5:6])
+    ig_final(CHUNKS[6:])
     for chunk in CHUNKS[:6]:
         got.pop(("twin", chunk)).wait_recv()
     for half in range(2):
         cols = slice(half * width, (half + 1) * width)
         total[:, cols] = jnp.dot(
             a_t[:, 0:1536], grads[0:6, :, :, cols].reshape(1536, width), preferred_element_type=F32)
-    ig_final(CHUNKS[6:])
     for chunk in CHUNKS[6:]:
         got.pop(("twin", chunk)).wait_recv()
     outs = []

time: 62.8 us -> 62.3 us (level)
  no operation moved by 1% of the time
where the time goes in v5:
time: 62.3 us; the launch traced here: 62.1 us
  Pallas kernels  61.5 us (99%)
  between operations  0.64 us (1%)
    pallas_call x1, Pallas kernels, body(): pl.pallas_call(functools.partial(kernel, float(tokens * n_dp) ** (-0.5)),...  59.5 us
    pallas_call x1, Pallas kernels, body(): pl.pallas_call(place, out_shape=tuple((jax.ShapeDtypeStruct(r.shape, r.dt...  2 us

profile of v5, /device:TPU:1, one launch (start us, length us, event | category | flops | bytes accessed | tf_op | source)
XLA Modules:
  0.0 62.1 jit_solution(9031073357803647443)
XLA Ops:
  0.6 59.5 %shard_map.85 = (bf16[8,4096]{1,0:T(8,128)(2,1)}, bf16[256,896]{1,0:T(8,128)(2,1)}, bf16[256,896]{1,0:T(8,128)(2,1)}) custom-call(bf16[8,4096]{1,0:T(8,128)(2,1)} %act_hbm.1, bf16[128,896]{1,0:T(8,128)(2,1)} %gate_hbm.1, bf16[128,896]{1,0:T(8,128)(2,1)} %up_hbm.1, bf16[128,896]{1,0:T(8,128)(2,1)} %hidden_hbm.1, bf16[256,896]{1,0:T(8,128)(2,1)} %wgate_hbm.1, ...), custom_call_target="tpu_custom_call" | custom-call | flops 3758096384 | bytes 4500000 | tf_op jit(solution)/shard_map/pallas_call | solution.py:358
  60.1 2.0 %shard_map.86 = (bf16[8,4096]{1,0:T(8,128)(2,1)}, bf16[256,896]{1,0:T(8,128)(2,1)}, bf16[256,896]{1,0:T(8,128)(2,1)}) custom-call(bf16[8,4096]{1,0:T(8,128)(2,1)} %get-tuple-element.6.a_in, bf16[256,896]{1,0:T(8,128)(2,1)} %get-tuple-element.7.b_in, bf16[256,896]{1,0:T(8,128)(2,1)} %get-tuple-element.8.c_in), custom_call_target="tpu_custom_call" | custom-call | tf_op jit(solution)/shard_map/pallas_call | solution.py:399

commit v6 on v5

--- a/solution.py
+++ b/solution.py
@@ -248,10 +248,10 @@
 
     sent = [0]
 
-    def drain():
-        for copy in copies[sent[0]:]:
+    def drain(upto):
+        for copy in copies[sent[0]:upto]:
             copy.wait_send()
-        sent[0] = len(copies)
+        sent[0] = upto
 
     on_even(0)
     on_odd(1)
@@ -335,7 +335,7 @@
             a_t[:, 1536:2048], grads[6:8, :, :, cols].reshape(512, width), preferred_element_type=F32)
         ) * grad_scale).astype(BF16)
         outs.append(load(out_buf.at[half], out_hbm))
-    drain()
+    drain(len(copies) // 2)
     assert not got
     for copy in f_copies:
         copy.wait_recv()
@@ -344,6 +344,7 @@
         at = pl.ds(pl.multiple_of(((index % 2 + core) % 2) * 8, 8), 8)
         igrad[:, index * 256:(index + 1) * 256] = f_recv[rel, at].astype(BF16)
     outs.append(load(igrad, igrad_hbm))
+    drain(len(copies))
     for copy in outs:
         copy.wait()
 

time: 62.3 us -> 62.3 us (level)
  no operation moved by 1% of the time
where the time goes in v6:
time: 62.3 us; the launch traced here: 62.1 us
  Pallas kernels  61.5 us (99%)
  between operations  0.64 us (1%)
    pallas_call x1, Pallas kernels, body(): pl.pallas_call(functools.partial(kernel, float(tokens * n_dp) ** (-0.5)),...  59.5 us
    pallas_call x1, Pallas kernels, body(): pl.pallas_call(place, out_shape=tuple((jax.ShapeDtypeStruct(r.shape, r.dt...  2 us

profile of v6, /device:TPU:1, one launch (start us, length us, event | category | flops | bytes accessed | tf_op | source)
XLA Modules:
  0.0 62.1 jit_solution(15500070370709106080)
XLA Ops:
  0.6 59.5 %shard_map.85 = (bf16[8,4096]{1,0:T(8,128)(2,1)}, bf16[256,896]{1,0:T(8,128)(2,1)}, bf16[256,896]{1,0:T(8,128)(2,1)}) custom-call(bf16[8,4096]{1,0:T(8,128)(2,1)} %act_hbm.1, bf16[128,896]{1,0:T(8,128)(2,1)} %gate_hbm.1, bf16[128,896]{1,0:T(8,128)(2,1)} %up_hbm.1, bf16[128,896]{1,0:T(8,128)(2,1)} %hidden_hbm.1, bf16[256,896]{1,0:T(8,128)(2,1)} %wgate_hbm.1, ...), custom_call_target="tpu_custom_call" | custom-call | flops 3758096384 | bytes 4500000 | tf_op jit(solution)/shard_map/pallas_call | solution.py:359
  60.1 2.0 %shard_map.86 = (bf16[8,4096]{1,0:T(8,128)(2,1)}, bf16[256,896]{1,0:T(8,128)(2,1)}, bf16[256,896]{1,0:T(8,128)(2,1)}) custom-call(bf16[8,4096]{1,0:T(8,128)(2,1)} %get-tuple-element.6.a_in, bf16[256,896]{1,0:T(8,128)(2,1)} %get-tuple-element.7.b_in, bf16[256,896]{1,0:T(8,128)(2,1)} %get-tuple-element.8.c_in), custom_call_target="tpu_custom_call" | custom-call | tf_op jit(solution)/shard_map/pallas_call | solution.py:400
